TPU v7x, 32 devices: a whole 2x2x4 slice. The times are simulated.
32 devices in a mesh: samp: 16 (over z, y, x), trait: 2 (over core).
Axes of the slice: x: 2, y: 2, z: 4, core: 2. Of those that a mesh axis runs over, the one named last changes fastest.
Arguments:
- samples: bfloat16 [8192, 2048], P('samp'), may hold values from -18 to 18
- traits: bfloat16 [8192, 2048], P('samp', 'trait'), may hold values from -6 to 6
- whitening: bfloat16 [2048, 2048], P(None, 'trait'), may hold values from -0.0017089844 to 0.0017089844
- singular: float32 [2048], replicated, may hold values from 0.3 to 3
- lambdas: float32 [4], replicated, may hold values from 0.1 to 10
Outputs:
- loo_residual: float32 [4, 8192, 2048], P(None, 'samp', 'trait')
All inputs are finite; a program needn't handle non-finite values.
Results may differ from a plain program's by a relative error of at most 0.0041.
Values may be sent and summed in bfloat16 or wider, within the bound.
A program may use at most 64 MiB of HBM per device.

v0:
```python
import jax
import jax.numpy as jnp
from jax import lax
from jax.sharding import PartitionSpec as P


def local(samples, traits, whitening, singular, lambdas):
    squared_values = singular * singular
    shrink = squared_values[:, None] / (squared_values[:, None] + lambdas[None, :])
    own_components = jnp.dot(samples, whitening, preferred_element_type=jnp.float32).astype(
        jnp.bfloat16
    )
    components = lax.all_gather(own_components, "trait", axis=1, tiled=True)
    wide_float = components.astype(jnp.float32)
    leverage = jnp.dot(wide_float * wide_float, shrink, precision=lax.Precision.HIGHEST)
    contract_rows = (((0,), (0,)), ((), ()))
    partial_share = lax.psum_scatter(
        lax.dot_general(components, traits, contract_rows, preferred_element_type=jnp.float32),
        "samp",
        scatter_dimension=0,
        tiled=True,
    )
    projected = lax.all_gather(partial_share.astype(jnp.bfloat16), "samp", axis=0, tiled=True)
    scaled = (shrink.T[:, :, None] * projected.astype(jnp.float32)[None]).astype(jnp.bfloat16)
    fitted = jnp.einsum("np,lpt->lnt", components, scaled, preferred_element_type=jnp.float32)
    divisor = jnp.maximum(1.0 - leverage.T[:, :, None], 0.25)
    return (traits.astype(jnp.float32)[None] - fitted) / divisor


def solution(mesh):
    return jax.shard_map(
        local,
        mesh=mesh,
        in_specs=(P("samp", None), P("samp", "trait"), P(None, "trait"), P(), P()),
        out_specs=P(None, "samp", "trait"),
        check_vma=False,
    )
```

profile of v0, /device:TPU:0, one launch (start us, length us, event | category | flops | bytes accessed | tf_op | source)
XLA Modules:
  0.0 346.0 jit_solution(4382076710610286796)
XLA Ops:
  6.5 0.0 copy-start
  6.5 0.0 all-gather.3.cloned.1.call-start
  6.5 1.6 copy-done
  8.1 5.5 %convolution_convert_fusion = bf16[512,1024]{1,0:T(8,128)(2,1)} fusion(bf16[512,2048]{1,0:T(8,128)(2,1)S(1)} %copy-done, bf16[2048,1024]{1,0:T(8,128)(2,1)} %param.7), kind=kOutput, calls=%fused_computation.10 | convolution fusion | flops 2148007936 | bytes 7340032 | tf_op jit(solution)/shard_map/dot_general | solution.py:10
  13.6 0.0 all-gather.3.cloned.1.call-update
  13.6 0.0 reduce-scatter.2.cloned.1.call-start
  13.7 13.4 %all-gather.3.cloned.1.call-done = bf16[512,2048]{1,0:T(8,128)(2,1)} async-done(((bf16[512,1024]{1,0:T(8,128)(2,1)}), bf16[512,2048]{1,0:T(8,128)(2,1)}) %all-gather.3.cloned.1.call-update) | async-done | bytes 2097168 | tf_op jit(solution)/shard_map/all_gather | solution.py:13
  27.1 0.0 copy-done.2
  27.1 7.4 %fusion.18 = f32[2048,1024]{0,1:T(8,128)} fusion(bf16[512,2048]{1,0:T(8,128)(2,1)} %all-gather.3.cloned.1.call-done, bf16[512,1024]{1,0:T(8,128)(2,1)S(1)} %copy-done.2), kind=kOutput, calls=%fused_computation.18 | convolution fusion | flops 2147483648 | bytes 11534336 | tf_op jit(solution)/shard_map/dot_general | solution.py:18
  34.4 0.0 reduce-scatter.2.cloned.1.call-update
  34.5 0.0 copy-start.3
  34.5 0.0 copy-start.4
  34.5 0.2 all-gather.5.cloned.1.call-start
  34.7 178.9 %reduce-scatter.2.cloned.1.call-done = f32[128,1024]{0,1:T(8,128)} async-done(((f32[2048,1024]{0,1:T(8,128)}), f32[128,1024]{0,1:T(8,128)}) %reduce-scatter.2.cloned.1.call-update) | async-done | bytes 524304 | tf_op jit(solution)/shard_map/reduce_scatter | solution.py:17
  213.6 1.8 convert_element_type.20
  215.4 0.0 all-gather.5.cloned.1.call-update
  215.4 1.6 copy.6
  217.1 0.0 copy-done.3
  217.1 0.1 add_divide_fusion
  217.2 5.5 %fusion.11 = f32[4,512]{1,0:T(4,128)S(1)} fusion(bf16[512,2048]{1,0:T(8,128)(2,1)} %all-gather.3.cloned.1.call-done, f32[4]{0:T(128)S(1)} %copy-done.4, f32[2048]{0:T(1024)S(1)} %mul.19), kind=kOutput, calls=%fused_computation.12 | convolution fusion | flops 52449280 | bytes 2113552 | tf_op jit(solution)/shard_map/dot_general | solution.py:15
  222.7 85.3 %all-gather.5.cloned.1.call-done = bf16[2048,1024]{0,1:T(8,128)(2,1)} async-done(((bf16[128,1024]{0,1:T(8,128)(2,1)}), bf16[2048,1024]{0,1:T(8,128)(2,1)}) %all-gather.5.cloned.1.call-update) | async-done | bytes 4194320 | tf_op jit(solution)/shard_map/all_gather | solution.py:23
  308.0 6.8 %convert_element_type.21 = f32[2048,1024]{0,1:T(8,128)} convert(bf16[2048,1024]{0,1:T(8,128)(2,1)} %all-gather.5.cloned.1.call-done) | non-fusion elementwise | flops 2097152 | bytes 12582912 | tf_op jit(solution)/shard_map/convert_element_type | solution.py:24
  314.8 16.0 %fusion.3 = f32[4,512,1024]{1,2,0:T(8,128)} fusion(f32[4,512]{1,0:T(4,128)S(1)} %fusion.11, f32[512,1024]{0,1:T(8,128)S(1)} %copy-done.1, f32[2048,1024]{0,1:T(8,128)} %convert_element_type.21, f32[4,2048]{1,0:T(4,128)S(1)} %add_divide_fusion, bf16[512,2048]{1,0:T(8,128)(2,1)} %all-gather.3.cloned.1.call-done), kind=kOutput, calls=%fused_computation.5 | convolution fusion | flops 8610906112 | bytes 21012480 | tf_op jit(solution)/shard_map/np,lpt->lnt/dot_general | solution.py:25
  330.8 8.7 %copy.7 = f32[4,512,1024]{2,1,0:T(8,128)} copy(f32[4,512,1024]{1,2,0:T(8,128)} %fusion.3) | data formatting | bytes 16777216 | tf_op jit(solution)/shard_map/div | solution.py:27
  (5 shorter events, 0.0 us)
Async XLA Ops:
  6.5 1.6 copy-start
  6.5 20.5 %copy-start.2 = (bf16[512,1024]{1,0:T(8,128)(2,1)S(1)}, bf16[512,1024]{1,0:T(8,128)(2,1)}, u32[]{:S(2)}) copy-start(bf16[512,1024]{1,0:T(8,128)(2,1)} %param.6) | copy-start | bytes 3145732
  6.5 20.5 %all-gather.3.cloned.1.call-start = ((), (), s32[]{:S(2)}) async-start(), calls=%async_computation.1 | async-start | bytes 3145728 | tf_op jit(solution)/shard_map/all_gather | solution.py:13
  13.6 200.0 %reduce-scatter.2.cloned.1.call-start = ((), (), s32[]{:S(2)}) async-start(), calls=%async_computation.2 | async-start | bytes 8912896 | tf_op jit(solution)/shard_map/reduce_scatter | solution.py:17
  34.5 182.6 %copy-start.3 = (f32[2048]{0:T(1024)S(1)}, f32[2048]{0:T(1024)}, u32[]{:S(2)}) copy-start(f32[2048]{0:T(1024)} %param.8) | copy-start | bytes 24580
  34.5 182.6 %copy-start.4 = (f32[4]{0:T(128)S(1)}, f32[4]{0:T(128)}, u32[]{:S(2)}) copy-start(f32[4]{0:T(128)} %param.9) | copy-start | bytes 52
  34.5 273.5 %all-gather.5.cloned.1.call-start = ((), (), s32[]{:S(2)}) async-start(), calls=%async_computation.3 | async-start | bytes 4456448 | tf_op jit(solution)/shard_map/all_gather | solution.py:23
  308.0 6.8 %copy-start.1 = (f32[512,1024]{0,1:T(8,128)S(1)}, f32[512,1024]{0,1:T(8,128)}, u32[]{:S(2)}) copy-start(f32[512,1024]{0,1:T(8,128)} %copy.6) | copy-start | bytes 6291460
Sparse Core Ops, SparseCore 0:
  13.8 13.2 all-gather.2
  34.6 178.9 reduce-scatter.1
  216.3 91.5 all-gather.4
where the time goes:
time: 346 us
  waiting for transfers between devices  278 us (80%)
  matrix products  34.4 us (10%)
  between operations  13.1 us (4%)
  local copies, waits for them, and re-layouts  11.9 us (3%)
  other arithmetic  8.66 us (3%)
    reduce_scatter x1, waiting for transfers between devices, local(): lax.psum_scatter(lax.dot_general(components, traits, contract_rows, prefe...  179 us
    all_gather x1, waiting for transfers between devices, local(): lax.all_gather(partial_share.astype(jnp.bfloat16), 'samp', axis=0, tiled=...  85.3 us
    dot_general x1, matrix products, local(): jnp.einsum('np,lpt->lnt', components, scaled, preferred_element_type=jnp....  16 us
    all_gather x1, waiting for transfers between devices, local(): components = lax.all_gather(own_components, 'trait', axis=1, tiled=True)  13.4 us
    div x1, local copies, waits for them, and re-layouts, local(): return (traits.astype(jnp.float32)[None] - fitted) / divisor  8.67 us
    dot_general x1, matrix products, local(): lax.dot_general(components, traits, contract_rows, preferred_element_type...  7.37 us
  transfers between devices with their start and end apart: 3, of which 3 were waited for; matrix products, arithmetic and copies ran while one was open for 2% of the time, Pallas kernels for 0%

commit v1 on v0

v1 whole, which is shorter than its diff:
```python
import functools

import jax
import jax.numpy as jnp
from jax import lax
from jax.experimental import pallas as pl
from jax.experimental.pallas import tpu as pltpu
from jax.sharding import PartitionSpec as P

MESH = pl.DeviceIdType.MESH
F32 = jnp.float32
BF16 = jnp.bfloat16
LANES = 128
ROWS = 16


def bit_orders(bits):
    rest = list(range(bits))
    if bits < 3:
        return [rest, rest[::-1]]
    a, b = rest, [1, 0] + rest[2:]
    c, d = [2, 0, 1] + rest[3:], [2, 1, 0] + rest[3:]
    return [a, b, c, a, b, d, a, b]


def exchange_kernel(
    n, nt, nl,
    s_ref, w_ref, y_ref, sing_ref, lam_ref,
    c_ref, pj_ref, lev_ref, shr_ref,
    acc, pb, rb, rs_send, rs_recv, ag_send, ag_recv, c_send, c_recv,
):
    bits = n.bit_length() - 1
    units, unit, _ = acc.shape
    own_k = c_ref.shape[2]
    own = own_k // unit
    orders = bit_orders(bits)
    me, mt = lax.axis_index("samp"), lax.axis_index("trait")
    value = [lax.rem(lax.div(me, 1 << b), 2) for b in range(bits)]
    peer = [me + (1 - 2 * value[b]) * (1 << b) for b in range(bits)]
    others = [lax.rem(mt + d, nt) for d in range(1, nt)]

    barrier = pltpu.get_barrier_semaphore()
    for p in peer:
        pl.semaphore_signal(barrier, inc=1, device_id=(p, mt), device_id_type=MESH)
    for t in others:
        pl.semaphore_signal(barrier, inc=1, device_id=(me, t), device_id_type=MESH)

    def rows(start, size):
        return pl.ds(pl.multiple_of(start, ROWS), size)

    def order(s):
        return orders[s % len(orders)]

    keep, give = [], []
    for s in range(units):
        start, keeps, gives = 0, [], []
        for j, b in enumerate(order(s)):
            size = unit >> (j + 1)
            keeps.append(start + value[b] * size)
            gives.append(start + (1 - value[b]) * size)
            start = keeps[-1]
        keep.append(keeps)
        give.append(gives)

    def place(s):
        if own:
            return lax.rem(mt + s // own, nt) * own + s % own
        return s

    def rs_copy(s, j):
        size = unit >> (j + 1)
        return pltpu.make_async_remote_copy(
            src_ref=pb.at[s, rows(give[s][j], size)],
            dst_ref=rb.at[s, pl.ds(unit - (unit >> j), size)],
            send_sem=rs_send.at[s, j],
            recv_sem=rs_recv.at[s, j],
            device_id=(peer[order(s)[j]], mt),
            device_id_type=MESH,
        )

    def ag_copy(s, j):
        size = unit >> (j + 1)
        held = pj_ref.at[place(s), rows(keep[s][j], size)]
        return pltpu.make_async_remote_copy(
            src_ref=held,
            dst_ref=held,
            send_sem=ag_send.at[s, j],
            recv_sem=ag_recv.at[s, j],
            device_id=(peer[order(s)[j]], mt),
            device_id_type=MESH,
        )

    def c_copy(d):
        return pltpu.make_async_remote_copy(
            src_ref=c_ref.at[mt],
            dst_ref=c_ref.at[mt],
            send_sem=c_send.at[d],
            recv_sem=c_recv.at[d],
            device_id=(me, others[d]),
            device_id_type=MESH,
        )

    contract_rows = (((0,), (0,)), ((), ()))

    def project(s):
        if own:
            t = lax.rem(mt + s // own, nt)
            part = c_ref[t, :, (s % own) * unit:(s % own + 1) * unit]
            acc[s] = lax.dot_general(part, y_ref[...], contract_rows, preferred_element_type=F32)
        else:
            pieces = unit // own_k
            for i in range(pieces):
                acc[s, i * own_k:(i + 1) * own_k, :] = lax.dot_general(
                    c_ref[s * pieces + i], y_ref[...], contract_rows, preferred_element_type=F32
                )
        size = unit >> 1
        pb[s, rows(give[s][0], size), :] = acc[s, rows(give[s][0], size), :].astype(BF16)

    block = min(unit, own_k)
    for q in range(own_k // block):
        cols = slice(q * block, (q + 1) * block)
        c_ref[mt, :, cols] = jnp.dot(
            s_ref[...], w_ref[:, cols], preferred_element_type=F32
        ).astype(BF16)
        if own:
            project(q)
        if q == 0:
            pl.semaphore_wait(barrier, bits + nt - 1)
        if own:
            rs_copy(q, 0).start()
    for d in range(nt - 1):
        c_copy(d).start()
    for d in range(nt - 1):
        c_copy(d).wait_recv()
    for s in range(own, units):
        project(s)
        rs_copy(s, 0).start()

    for j in range(bits):
        size = unit >> (j + 1)
        base = unit - (unit >> j)
        for s in range(units):
            rs_copy(s, j).wait_recv()
            if j + 1 < bits:
                half = size >> 1
                first = give[s][j + 1]
                landed = rb[s, rows(base + first - keep[s][j], half), :].astype(F32)
                pb[s, rows(first, half), :] = (acc[s, rows(first, half), :] + landed).astype(BF16)
                rs_copy(s, j + 1).start()
                second = keep[s][j + 1]
                landed = rb[s, rows(base + second - keep[s][j], half), :].astype(F32)
                acc[s, rows(second, half), :] = acc[s, rows(second, half), :] + landed
            else:
                total = acc[s, rows(keep[s][j], size), :] + rb[s, base:base + size, :].astype(F32)
                pj_ref[place(s), rows(keep[s][j], size), :] = total.astype(BF16)
                ag_copy(s, j).start()

    for j in range(bits - 2, -1, -1):
        for s in range(units):
            ag_copy(s, j + 1).wait_recv()
            ag_copy(s, j).start()

    squared = sing_ref[...] * sing_ref[...]
    row = lax.broadcasted_iota(jnp.int32, (LANES, squared.shape[1]), 0)
    lam = jnp.full(row.shape, 1.0, F32)
    for l in range(nl):
        lam = jnp.where(row == l, lam_ref[l], lam)
    shrink = squared / (squared + lam)
    shr_ref[...] = shrink.T
    tall = c_ref.shape[1]
    step = min(64, tall)

    @pl.loop(0, tall // step)
    def _(i):
        here = pl.ds(pl.multiple_of(i * step, step), step)
        sums = [jnp.zeros((step, 1), F32) for _ in range(nl)]
        for t in range(nt):
            wide = c_ref[t, here, :].astype(F32)
            wide = wide * wide
            for l in range(nl):
                weight = shrink[l:l + 1, t * own_k:(t + 1) * own_k]
                sums[l] = sums[l] + jnp.sum(wide * weight, axis=1, keepdims=True)
        lane = lax.broadcasted_iota(jnp.int32, (step, LANES), 1)
        result = jnp.zeros((step, LANES), F32)
        for l in range(nl):
            result = jnp.where(lane == l, sums[l], result)
        lev_ref[here, :] = result

    for s in range(units):
        ag_copy(s, 0).wait_recv()
    for d in range(nt - 1):
        c_copy(d).wait_send()
    for s in range(units):
        for j in range(bits):
            rs_copy(s, j).wait_send()
            ag_copy(s, j).wait_send()


def fit_kernel(nl, nt, c_ref, pj_ref, shr_ref, lev_ref, y_ref, out_ref):
    own_k = c_ref.shape[2]
    target = y_ref[...].astype(F32)
    for l in range(nl):
        fitted = jnp.zeros(target.shape, F32)
        for t in range(nt):
            here = slice(t * own_k, (t + 1) * own_k)
            wide = pj_ref[here, :].astype(F32)
            scaled = (shr_ref[here, l:l + 1] * wide).astype(BF16)
            fitted = fitted + jnp.dot(c_ref[t], scaled, preferred_element_type=F32)
        divisor = jnp.maximum(1.0 - lev_ref[:, l:l + 1], 0.25)
        out_ref[l] = (target - fitted) * (1.0 / divisor)


def local(n, nt, samples, traits, whitening, singular, lambdas):
    tall, k = samples.shape
    own_k = whitening.shape[1]
    wide = traits.shape[1]
    nl = lambdas.shape[0]
    bits = n.bit_length() - 1
    unit = ROWS << bits
    units = k // unit
    vmem = pl.BlockSpec(memory_space=pltpu.VMEM)
    components, projected, leverage, shrink = pl.pallas_call(
        functools.partial(exchange_kernel, n, nt, nl),
        out_shape=[
            jax.ShapeDtypeStruct((nt, tall, own_k), BF16),
            jax.ShapeDtypeStruct((units, unit, wide), BF16),
            jax.ShapeDtypeStruct((tall, LANES), F32),
            jax.ShapeDtypeStruct((k, LANES), F32),
        ],
        in_specs=[vmem] * 4 + [pl.BlockSpec(memory_space=pltpu.SMEM)],
        out_specs=[vmem] * 4,
        scratch_shapes=[
            pltpu.VMEM((units, unit, wide), F32),
            pltpu.VMEM((units, unit, wide), BF16),
            pltpu.VMEM((units, unit, wide), BF16),
            pltpu.SemaphoreType.DMA((units, bits)),
            pltpu.SemaphoreType.DMA((units, bits)),
            pltpu.SemaphoreType.DMA((units, bits)),
            pltpu.SemaphoreType.DMA((units, bits)),
            pltpu.SemaphoreType.DMA((nt - 1,)),
            pltpu.SemaphoreType.DMA((nt - 1,)),
        ],
        compiler_params=pltpu.CompilerParams(
            collective_id=0, has_side_effects=True, vmem_limit_bytes=56 * 2**20
        ),
        name="project_and_sum",
    )(samples, whitening, traits, singular.reshape(1, k), lambdas)
    projected = projected.reshape(k, wide)
    tile = min(256, wide)
    return pl.pallas_call(
        functools.partial(fit_kernel, nl, nt),
        grid=(wide // tile,),
        out_shape=jax.ShapeDtypeStruct((nl, tall, wide), F32),
        in_specs=[
            pl.BlockSpec((nt, tall, own_k), lambda i: (0, 0, 0)),
            pl.BlockSpec((k, tile), lambda i: (0, i)),
            pl.BlockSpec((k, LANES), lambda i: (0, 0)),
            pl.BlockSpec((tall, LANES), lambda i: (0, 0)),
            pl.BlockSpec((tall, tile), lambda i: (0, i)),
        ],
        out_specs=pl.BlockSpec((nl, tall, tile), lambda i: (0, 0, i)),
        compiler_params=pltpu.CompilerParams(vmem_limit_bytes=48 * 2**20),
        name="fit",
    )(components, projected, shrink, leverage, traits)


def solution(mesh):
    n, nt = mesh.shape["samp"], mesh.shape["trait"]
    return jax.shard_map(
        functools.partial(local, n, nt),
        mesh=mesh,
        in_specs=(P("samp", None), P("samp", "trait"), P(None, "trait"), P(), P()),
        out_specs=P(None, "samp", "trait"),
        check_vma=False,
    )
```

time: 346 us -> 119 us (0.34)
  waiting for transfers between devices: 278 us -> 0 us
  Pallas kernels: 0 us -> 115 us
  matrix products: 34.4 us -> 0 us
  between operations: 13.1 us -> 0.03 us
  other arithmetic: 8.66 us -> 0 us
  local copies, waits for them, and re-layouts: 11.9 us -> 3.76 us
    reduce_scatter x1 -> x0, waiting for transfers between devices: 179 us -> none  [local(): lax.psum_scatter(lax.dot_general(components, traits, contract_rows, prefe...]
    pallas_call x0 -> x2, Pallas kernels: none -> 115 us  [the longest x1 102 us: local(): pl.pallas_call(functools.partial(exchange_kernel, n, nt, nl), out_shape=[...]
    all_gather x2 -> x0, waiting for transfers between devices: 98.7 us -> none  [the longest x1 85.3 us: local(): lax.all_gather(partial_share.astype(jnp.bfloat16), 'samp', axis=0, tiled=...]
    dot_general x4 -> x0, matrix products: 34.4 us -> none  [the longest x1 16 us: local(): jnp.einsum('np,lpt->lnt', components, scaled, preferred_element_type=jnp....]
    div x1 -> x0, local copies, waits for them, and re-layouts: 8.67 us -> none  [local(): return (traits.astype(jnp.float32)[None] - fitted) / divisor]
    convert_element_type x2 -> x0, other arithmetic: 8.57 us -> none  [the longest x1 6.8 us: local(): projected.astype(jnp.float32)[None]]
  transfers between devices with their start and end apart: 3 -> 0, of which waited for: 3 -> 0; matrix products, arithmetic and copies ran while one was open for 2% -> 0% of each run, Pallas kernels for 0% -> 0%
where the time goes in v1:
time: 119 us
  Pallas kernels  115 us (97%)
  local copies, waits for them, and re-layouts  3.76 us (3%)
    pallas_call x1, Pallas kernels, local(): pl.pallas_call(functools.partial(exchange_kernel, n, nt, nl), out_shape=[...  102 us
    pallas_call x1, Pallas kernels, local(): pl.pallas_call(functools.partial(fit_kernel, nl, nt), grid=(wide // tile,...  13 us
    unnamed x8, local copies, waits for them, and re-layouts  3.76 us

profile of v1, /device:TPU:0, one launch (start us, length us, event | category | flops | bytes accessed | tf_op | source)
XLA Modules:
  0.0 118.8 jit_solution(16925621238937657884)
XLA Ops:
  0.0 0.0 copy-start
  0.0 102.0 %project_and_sum.1 = (bf16[2,512,1024]{2,1,0:T(8,128)(2,1)}, bf16[8,256,1024]{2,1,0:T(8,128)(2,1)}, f32[512,128]{1,0:T(8,128)}, f32[2048,128]{1,0:T(8,128)}) custom-call(bf16[512,2048]{1,0:T(8,128)(2,1)} %s_ref.1, bf16[2048,1024]{1,0:T(8,128)(2,1)} %w_ref.1, bf16[512,1024]{1,0:T(8,128)(2,1)} %y_ref.3, f32[1,2048]{1,0:T(1,128)} %bitcast.3, f32[4]{0:T(128)} %lam_ref.1), custom_call_target="tpu_custom_call" | custom-call | tf_op jit(solution)/shard_map/project_and_sum/pallas_call | solution.py:222
  102.0 0.0 copy-done
  102.0 0.0 copy-start.1
  102.0 1.6 %copy-done.1 = bf16[2,512,1024]{2,1,0:T(8,128)(2,1)S(1)} copy-done((bf16[2,512,1024]{2,1,0:T(8,128)(2,1)S(1)}, bf16[2,512,1024]{2,1,0:T(8,128)(2,1)}, u32[]{:S(2)}) %copy-start.1) | copy-done | bytes 2097176
  103.6 0.0 copy-start.2
  103.6 1.2 %copy-done.2 = f32[2048,128]{1,0:T(8,128)S(1)} copy-done((f32[2048,128]{1,0:T(8,128)S(1)}, f32[2048,128]{1,0:T(8,128)}, u32[]{:S(2)}) %copy-start.2) | copy-done | bytes 1048600
  104.8 0.0 copy-start.3
  104.8 0.9 copy-done.3
  105.8 13.0 %fit.1 = f32[4,512,1024]{2,1,0:T(8,128)} custom-call(bf16[2,512,1024]{2,1,0:T(8,128)(2,1)S(1)} %copy-done.1, bf16[2048,1024]{1,0:T(8,128)(2,1)} %bitcast.2, f32[2048,128]{1,0:T(8,128)S(1)} %copy-done.2, f32[512,128]{1,0:T(8,128)S(1)} %copy-done.3, bf16[512,1024]{1,0:T(8,128)(2,1)S(1)} %copy-done), custom_call_target="tpu_custom_call" | custom-call | tf_op jit(solution)/shard_map/fit/pallas_call | solution.py:250
Async XLA Ops:
  0.0 102.0 %copy-start = (bf16[512,1024]{1,0:T(8,128)(2,1)S(1)}, bf16[512,1024]{1,0:T(8,128)(2,1)}, u32[]{:S(2)}) copy-start(bf16[512,1024]{1,0:T(8,128)(2,1)} %y_ref.3) | copy-start | bytes 3145732
  102.0 1.6 %copy-start.1 = (bf16[2,512,1024]{2,1,0:T(8,128)(2,1)S(1)}, bf16[2,512,1024]{2,1,0:T(8,128)(2,1)}, u32[]{:S(2)}) copy-start(bf16[2,512,1024]{2,1,0:T(8,128)(2,1)} %get-tuple-element.9.c_ref) | copy-start | bytes 6291460
  103.6 1.2 %copy-start.2 = (f32[2048,128]{1,0:T(8,128)S(1)}, f32[2048,128]{1,0:T(8,128)}, u32[]{:S(2)}) copy-start(f32[2048,128]{1,0:T(8,128)} %get-tuple-element.11.shr_ref) | copy-start | bytes 3145732
  104.8 0.9 copy-start.3

commit v2 on v1

--- a/solution.py
+++ b/solution.py
@@ -14,13 +14,15 @@
 ROWS = 16
 
 
+WAVE = 3
+
+
 def bit_orders(bits):
     rest = list(range(bits))
     if bits < 3:
         return [rest, rest[::-1]]
-    a, b = rest, [1, 0] + rest[2:]
-    c, d = [2, 0, 1] + rest[3:], [2, 1, 0] + rest[3:]
-    return [a, b, c, a, b, d, a, b]
+    a, b, c = [0, 1, 2] + rest[3:], [1, 2, 0] + rest[3:], [2, 0, 1] + rest[3:]
+    return [a, b, c, a, b, c, a, [1, 0, 2] + rest[3:]]
 
 
 def exchange_kernel(
@@ -117,77 +119,99 @@
         pb[s, rows(give[s][0], size), :] = acc[s, rows(give[s][0], size), :].astype(BF16)
 
     block = min(unit, own_k)
-    for q in range(own_k // block):
+
+    def own_block(q):
         cols = slice(q * block, (q + 1) * block)
         c_ref[mt, :, cols] = jnp.dot(
             s_ref[...], w_ref[:, cols], preferred_element_type=F32
         ).astype(BF16)
+        if q == own_k // block - 1:
+            if q == 0:
+                pl.semaphore_wait(barrier, bits + nt - 1)
+            for d in range(nt - 1):
+                c_copy(d).start()
+
+    def begin(s):
         if own:
-            project(q)
-        if q == 0:
+            if s < own:
+                own_block(s)
+            if s == own:
+                for d in range(nt - 1):
+                    c_copy(d).wait_recv()
+        elif s == 0:
+            for q in range(own_k // block):
+                own_block(q)
+            for d in range(nt - 1):
+                c_copy(d).wait_recv()
+        project(s)
+        if s == 0 and own_k > block:
             pl.semaphore_wait(barrier, bits + nt - 1)
-        if own:
-            rs_copy(q, 0).start()
-    for d in range(nt - 1):
-        c_copy(d).start()
-    for d in range(nt - 1):
-        c_copy(d).wait_recv()
-    for s in range(own, units):
-        project(s)
         rs_copy(s, 0).start()
 
-    for j in range(bits):
+    def halve(s, j):
         size = unit >> (j + 1)
         base = unit - (unit >> j)
-        for s in range(units):
-            rs_copy(s, j).wait_recv()
-            if j + 1 < bits:
-                half = size >> 1
-                first = give[s][j + 1]
-                landed = rb[s, rows(base + first - keep[s][j], half), :].astype(F32)
-                pb[s, rows(first, half), :] = (acc[s, rows(first, half), :] + landed).astype(BF16)
-                rs_copy(s, j + 1).start()
-                second = keep[s][j + 1]
-                landed = rb[s, rows(base + second - keep[s][j], half), :].astype(F32)
-                acc[s, rows(second, half), :] = acc[s, rows(second, half), :] + landed
-            else:
-                total = acc[s, rows(keep[s][j], size), :] + rb[s, base:base + size, :].astype(F32)
-                pj_ref[place(s), rows(keep[s][j], size), :] = total.astype(BF16)
-                ag_copy(s, j).start()
-
-    for j in range(bits - 2, -1, -1):
-        for s in range(units):
-            ag_copy(s, j + 1).wait_recv()
+        rs_copy(s, j).wait_recv()
+        if j + 1 < bits:
+            half = size >> 1
+            first = give[s][j + 1]
+            landed = rb[s, rows(base + first - keep[s][j], half), :].astype(F32)
+            pb[s, rows(first, half), :] = (acc[s, rows(first, half), :] + landed).astype(BF16)
+            rs_copy(s, j + 1).start()
+            second = keep[s][j + 1]
+            landed = rb[s, rows(base + second - keep[s][j], half), :].astype(F32)
+            acc[s, rows(second, half), :] = acc[s, rows(second, half), :] + landed
+        else:
+            total = acc[s, rows(keep[s][j], size), :] + rb[s, base:base + size, :].astype(F32)
+            pj_ref[place(s), rows(keep[s][j], size), :] = total.astype(BF16)
             ag_copy(s, j).start()
 
-    squared = sing_ref[...] * sing_ref[...]
-    row = lax.broadcasted_iota(jnp.int32, (LANES, squared.shape[1]), 0)
-    lam = jnp.full(row.shape, 1.0, F32)
-    for l in range(nl):
-        lam = jnp.where(row == l, lam_ref[l], lam)
-    shrink = squared / (squared + lam)
-    shr_ref[...] = shrink.T
-    tall = c_ref.shape[1]
-    step = min(64, tall)
-
-    @pl.loop(0, tall // step)
-    def _(i):
-        here = pl.ds(pl.multiple_of(i * step, step), step)
-        sums = [jnp.zeros((step, 1), F32) for _ in range(nl)]
-        for t in range(nt):
-            wide = c_ref[t, here, :].astype(F32)
-            wide = wide * wide
+    def double(s, j):
+        ag_copy(s, j).wait_recv()
+        if j > 0:
+            ag_copy(s, j - 1).start()
+
+    def leverage():
+        squared = sing_ref[...] * sing_ref[...]
+        row = lax.broadcasted_iota(jnp.int32, (LANES, squared.shape[1]), 0)
+        lam = jnp.full(row.shape, 1.0, F32)
+        for l in range(nl):
+            lam = jnp.where(row == l, lam_ref[l], lam)
+        shrink = squared / (squared + lam)
+        shr_ref[...] = shrink.T
+        tall = c_ref.shape[1]
+        step = min(64, tall)
+
+        @pl.loop(0, tall // step)
+        def _(i):
+            here = pl.ds(pl.multiple_of(i * step, step), step)
+            sums = [jnp.zeros((step, 1), F32) for _ in range(nl)]
+            for t in range(nt):
+                wide = c_ref[t, here, :].astype(F32)
+                wide = wide * wide
+                for l in range(nl):
+                    weight = shrink[l:l + 1, t * own_k:(t + 1) * own_k]
+                    sums[l] = sums[l] + jnp.sum(wide * weight, axis=1, keepdims=True)
+            lane = lax.broadcasted_iota(jnp.int32, (step, LANES), 1)
+            result = jnp.zeros((step, LANES), F32)
             for l in range(nl):
-                weight = shrink[l:l + 1, t * own_k:(t + 1) * own_k]
-                sums[l] = sums[l] + jnp.sum(wide * weight, axis=1, keepdims=True)
-        lane = lax.broadcasted_iota(jnp.int32, (step, LANES), 1)
-        result = jnp.zeros((step, LANES), F32)
-        for l in range(nl):
-            result = jnp.where(lane == l, sums[l], result)
-        lev_ref[here, :] = result
-
-    for s in range(units):
-        ag_copy(s, 0).wait_recv()
+                result = jnp.where(lane == l, sums[l], result)
+            lev_ref[here, :] = result
+
+    waves = [range(s, min(s + WAVE, units)) for s in range(0, units, WAVE)]
+    for k in range(2 * bits + len(waves)):
+        for w, wave in enumerate(waves):
+            for s in wave:
+                stage = k - w
+                if stage == 0:
+                    begin(s)
+                elif 0 < stage <= bits:
+                    halve(s, stage - 1)
+                elif bits < stage <= 2 * bits:
+                    double(s, 2 * bits - stage)
+        if k == 2 * bits - 1:
+            leverage()
+
     for d in range(nt - 1):
         c_copy(d).wait_send()
     for s in range(units):
@@ -259,7 +283,7 @@
             pl.BlockSpec((tall, tile), lambda i: (0, i)),
         ],
         out_specs=pl.BlockSpec((nl, tall, tile), lambda i: (0, 0, i)),
-        compiler_params=pltpu.CompilerParams(vmem_limit_bytes=48 * 2**20),
+        compiler_params=pltpu.CompilerParams(vmem_limit_bytes=60 * 2**20),
         name="fit",
     )(components, projected, shrink, leverage, traits)
 

time: 119 us -> 110 us (0.924)
  Pallas kernels: 115 us -> 109 us
  local copies, waits for them, and re-layouts: 3.76 us -> 0 us
    pallas_call x1, Pallas kernels: 102 us -> 95.3 us  [local(): pl.pallas_call(functools.partial(exchange_kernel, n, nt, nl), out_shape=[...]
    unnamed x8 -> x0, local copies, waits for them, and re-layouts: 3.76 us -> none
where the time goes in v2:
time: 110 us; the launch traced here: 109 us
  Pallas kernels  109 us (99%)
    pallas_call x1, Pallas kernels, local(): pl.pallas_call(functools.partial(exchange_kernel, n, nt, nl), out_shape=[...  95.3 us
    pallas_call x1, Pallas kernels, local(): pl.pallas_call(functools.partial(fit_kernel, nl, nt), grid=(wide // tile,...  14.2 us

profile of v2, /device:TPU:0, one launch (start us, length us, event | category | flops | bytes accessed | tf_op | source)
XLA Modules:
  0.0 109.5 jit_solution(10600431366736918107)
XLA Ops:
  0.0 95.3 %project_and_sum.1 = (bf16[2,512,1024]{2,1,0:T(8,128)(2,1)}, bf16[8,256,1024]{2,1,0:T(8,128)(2,1)}, f32[512,128]{1,0:T(8,128)}, f32[2048,128]{1,0:T(8,128)}) custom-call(bf16[512,2048]{1,0:T(8,128)(2,1)} %s_ref.1, bf16[2048,1024]{1,0:T(8,128)(2,1)} %w_ref.1, bf16[512,1024]{1,0:T(8,128)(2,1)} %y_ref.3, f32[1,2048]{1,0:T(1,128)} %bitcast.3, f32[4]{0:T(128)} %lam_ref.1), custom_call_target="tpu_custom_call" | custom-call | tf_op jit(solution)/shard_map/project_and_sum/pallas_call | solution.py:246
  95.3 14.2 %fit.1 = f32[4,512,1024]{2,1,0:T(8,128)} custom-call(bf16[2,512,1024]{2,1,0:T(8,128)(2,1)} %get-tuple-element.9.c_ref, bf16[2048,1024]{1,0:T(8,128)(2,1)} %bitcast.2, f32[2048,128]{1,0:T(8,128)} %get-tuple-element.11.shr_ref, f32[512,128]{1,0:T(8,128)} %get-tuple-element.12.lev_ref, bf16[512,1024]{1,0:T(8,128)(2,1)} %y_ref.3), custom_call_target="tpu_custom_call" | custom-call | tf_op jit(solution)/shard_map/fit/pallas_call | solution.py:274

commit v3 on v2

--- a/solution.py
+++ b/solution.py
@@ -14,7 +14,7 @@
 ROWS = 16
 
 
-WAVE = 3
+WAVE = 6
 
 
 def bit_orders(bits):
@@ -22,24 +22,39 @@
     if bits < 3:
         return [rest, rest[::-1]]
     a, b, c = [0, 1, 2] + rest[3:], [1, 2, 0] + rest[3:], [2, 0, 1] + rest[3:]
-    return [a, b, c, a, b, c, a, [1, 0, 2] + rest[3:]]
+    return [a, b, c] * 5 + [[1, 0, 2] + rest[3:]]
 
 
 def exchange_kernel(
-    n, nt, nl,
-    s_ref, w_ref, y_ref, sing_ref, lam_ref,
+    n, nt, nl, halves,
+    s_hbm, w_hbm, y_hbm, sing_ref, lam_ref,
     c_ref, pj_ref, lev_ref, shr_ref,
-    acc, pb, rb, rs_send, rs_recv, ag_send, ag_recv, c_send, c_recv,
+    s_ref, w_ref, y_ref, acc, pb, rb,
+    s_sem, w_sem, y_sem, rs_send, rs_recv, ag_send, ag_recv, c_send, c_recv,
 ):
     bits = n.bit_length() - 1
-    units, unit, _ = acc.shape
+    units, unit, cols_of_unit = acc.shape
     own_k = c_ref.shape[2]
     own = own_k // unit
+    block = min(unit, own_k)
+    blocks = own_k // block
     orders = bit_orders(bits)
     me, mt = lax.axis_index("samp"), lax.axis_index("trait")
     value = [lax.rem(lax.div(me, 1 << b), 2) for b in range(bits)]
     peer = [me + (1 - 2 * value[b]) * (1 << b) for b in range(bits)]
     others = [lax.rem(mt + d, nt) for d in range(1, nt)]
+
+    def w_copy(q):
+        cols = slice(q * block, (q + 1) * block)
+        return pltpu.make_async_copy(w_hbm.at[:, cols], w_ref.at[:, cols], w_sem.at[q])
+
+    s_copy = pltpu.make_async_copy(s_hbm, s_ref, s_sem)
+    y_copy = pltpu.make_async_copy(y_hbm, y_ref, y_sem)
+    s_copy.start()
+    w_copy(0).start()
+    y_copy.start()
+    for q in range(1, blocks):
+        w_copy(q).start()
 
     barrier = pltpu.get_barrier_semaphore()
     for p in peer:
@@ -64,10 +79,11 @@
         keep.append(keeps)
         give.append(gives)
 
-    def place(s):
+    def place(u):
+        s, h = u // halves, u % halves
         if own:
-            return lax.rem(mt + s // own, nt) * own + s % own
-        return s
+            s = lax.rem(mt + s // own, nt) * own + s % own
+        return s * halves + h
 
     def rs_copy(s, j):
         size = unit >> (j + 1)
@@ -104,49 +120,50 @@
 
     contract_rows = (((0,), (0,)), ((), ()))
 
-    def project(s):
+    def project(u):
+        s, h = u // halves, u % halves
+        right = y_ref[:, h * cols_of_unit:(h + 1) * cols_of_unit]
         if own:
             t = lax.rem(mt + s // own, nt)
             part = c_ref[t, :, (s % own) * unit:(s % own + 1) * unit]
-            acc[s] = lax.dot_general(part, y_ref[...], contract_rows, preferred_element_type=F32)
+            acc[u] = lax.dot_general(part, right, contract_rows, preferred_element_type=F32)
         else:
             pieces = unit // own_k
             for i in range(pieces):
-                acc[s, i * own_k:(i + 1) * own_k, :] = lax.dot_general(
-                    c_ref[s * pieces + i], y_ref[...], contract_rows, preferred_element_type=F32
+                acc[u, i * own_k:(i + 1) * own_k, :] = lax.dot_general(
+                    c_ref[s * pieces + i], right, contract_rows, preferred_element_type=F32
                 )
         size = unit >> 1
-        pb[s, rows(give[s][0], size), :] = acc[s, rows(give[s][0], size), :].astype(BF16)
-
-    block = min(unit, own_k)
+        pb[u, rows(give[u][0], size), :] = acc[u, rows(give[u][0], size), :].astype(BF16)
 
     def own_block(q):
         cols = slice(q * block, (q + 1) * block)
+        w_copy(q).wait()
         c_ref[mt, :, cols] = jnp.dot(
             s_ref[...], w_ref[:, cols], preferred_element_type=F32
         ).astype(BF16)
-        if q == own_k // block - 1:
-            if q == 0:
-                pl.semaphore_wait(barrier, bits + nt - 1)
+        if q == 0:
+            pl.semaphore_wait(barrier, bits + nt - 1)
+            y_copy.wait()
+        if q == blocks - 1:
             for d in range(nt - 1):
                 c_copy(d).start()
 
-    def begin(s):
-        if own:
-            if s < own:
+    def begin(u):
+        s, h = u // halves, u % halves
+        if u == 0:
+            s_copy.wait()
+        if h == 0:
+            if own and s < own:
                 own_block(s)
+            elif not own and s == 0:
+                for q in range(blocks):
+                    own_block(q)
             if s == own:
                 for d in range(nt - 1):
                     c_copy(d).wait_recv()
-        elif s == 0:
-            for q in range(own_k // block):
-                own_block(q)
-            for d in range(nt - 1):
-                c_copy(d).wait_recv()
-        project(s)
-        if s == 0 and own_k > block:
-            pl.semaphore_wait(barrier, bits + nt - 1)
-        rs_copy(s, 0).start()
+        project(u)
+        rs_copy(u, 0).start()
 
     def halve(s, j):
         size = unit >> (j + 1)
@@ -200,7 +217,7 @@
 
     waves = [range(s, min(s + WAVE, units)) for s in range(0, units, WAVE)]
     for k in range(2 * bits + len(waves)):
-        for w, wave in enumerate(waves):
+        for w, wave in reversed(list(enumerate(waves))):
             for s in wave:
                 stage = k - w
                 if stage == 0:
@@ -222,12 +239,13 @@
 
 def fit_kernel(nl, nt, c_ref, pj_ref, shr_ref, lev_ref, y_ref, out_ref):
     own_k = c_ref.shape[2]
+    pj = pj_ref[...].reshape(nt * own_k, pj_ref.shape[2])
     target = y_ref[...].astype(F32)
     for l in range(nl):
         fitted = jnp.zeros(target.shape, F32)
         for t in range(nt):
             here = slice(t * own_k, (t + 1) * own_k)
-            wide = pj_ref[here, :].astype(F32)
+            wide = pj[here, :].astype(F32)
             scaled = (shr_ref[here, l:l + 1] * wide).astype(BF16)
             fitted = fitted + jnp.dot(c_ref[t], scaled, preferred_element_type=F32)
         divisor = jnp.maximum(1.0 - lev_ref[:, l:l + 1], 0.25)
@@ -241,22 +259,32 @@
     nl = lambdas.shape[0]
     bits = n.bit_length() - 1
     unit = ROWS << bits
-    units = k // unit
+    halves = 2 if wide % (2 * LANES) == 0 else 1
+    cols = wide // halves
+    blocks = max(own_k // unit, 1)
+    rows = k // unit
+    units = rows * halves
     vmem = pl.BlockSpec(memory_space=pltpu.VMEM)
     components, projected, leverage, shrink = pl.pallas_call(
-        functools.partial(exchange_kernel, n, nt, nl),
+        functools.partial(exchange_kernel, n, nt, nl, halves),
         out_shape=[
             jax.ShapeDtypeStruct((nt, tall, own_k), BF16),
-            jax.ShapeDtypeStruct((units, unit, wide), BF16),
+            jax.ShapeDtypeStruct((units, unit, cols), BF16),
             jax.ShapeDtypeStruct((tall, LANES), F32),
             jax.ShapeDtypeStruct((k, LANES), F32),
         ],
-        in_specs=[vmem] * 4 + [pl.BlockSpec(memory_space=pltpu.SMEM)],
+        in_specs=[pl.BlockSpec(memory_space=pl.ANY)] * 3 + [vmem, pl.BlockSpec(memory_space=pltpu.SMEM)],
         out_specs=[vmem] * 4,
         scratch_shapes=[
-            pltpu.VMEM((units, unit, wide), F32),
-            pltpu.VMEM((units, unit, wide), BF16),
-            pltpu.VMEM((units, unit, wide), BF16),
+            pltpu.VMEM(samples.shape, BF16),
+            pltpu.VMEM(whitening.shape, BF16),
+            pltpu.VMEM(traits.shape, BF16),
+            pltpu.VMEM((units, unit, cols), F32),
+            pltpu.VMEM((units, unit, cols), BF16),
+            pltpu.VMEM((units, unit, cols), BF16),
+            pltpu.SemaphoreType.DMA,
+            pltpu.SemaphoreType.DMA((blocks,)),
+            pltpu.SemaphoreType.DMA,
             pltpu.SemaphoreType.DMA((units, bits)),
             pltpu.SemaphoreType.DMA((units, bits)),
             pltpu.SemaphoreType.DMA((units, bits)),
@@ -269,15 +297,16 @@
         ),
         name="project_and_sum",
     )(samples, whitening, traits, singular.reshape(1, k), lambdas)
-    projected = projected.reshape(k, wide)
-    tile = min(256, wide)
+    projected = projected.reshape(rows, halves, unit, cols)
+    tile = min(256, cols)
+    per = cols // tile
     return pl.pallas_call(
         functools.partial(fit_kernel, nl, nt),
         grid=(wide // tile,),
         out_shape=jax.ShapeDtypeStruct((nl, tall, wide), F32),
         in_specs=[
             pl.BlockSpec((nt, tall, own_k), lambda i: (0, 0, 0)),
-            pl.BlockSpec((k, tile), lambda i: (0, i)),
+            pl.BlockSpec((rows, None, unit, tile), lambda i: (0, i // per, 0, i % per)),
             pl.BlockSpec((k, LANES), lambda i: (0, 0)),
             pl.BlockSpec((tall, LANES), lambda i: (0, 0)),
             pl.BlockSpec((tall, tile), lambda i: (0, i)),

time: 110 us -> 105 us (0.955)
  Pallas kernels: 109 us -> 105 us
    pallas_call x1, Pallas kernels: 95.3 us -> 90.8 us  [local(): pl.pallas_call(functools.partial(exchange_kernel, n, nt, nl, halves), out...]
where the time goes in v3:
time: 105 us
  Pallas kernels  105 us (100%)
    pallas_call x1, Pallas kernels, local(): pl.pallas_call(functools.partial(exchange_kernel, n, nt, nl, halves), out...  90.8 us
    pallas_call x1, Pallas kernels, local(): pl.pallas_call(functools.partial(fit_kernel, nl, nt), grid=(wide // tile,...  14.3 us

profile of v3, /device:TPU:0, one launch (start us, length us, event | category | flops | bytes accessed | tf_op | source)
XLA Modules:
  0.0 105.1 jit_solution(17120110956899101354)
XLA Ops:
  0.0 90.8 %project_and_sum.1 = (bf16[2,512,1024]{2,1,0:T(8,128)(2,1)}, bf16[16,256,512]{2,1,0:T(8,128)(2,1)}, f32[512,128]{1,0:T(8,128)}, f32[2048,128]{1,0:T(8,128)}) custom-call(bf16[512,2048]{1,0:T(8,128)(2,1)} %s_hbm.1, bf16[2048,1024]{1,0:T(8,128)(2,1)} %w_hbm.1, bf16[512,1024]{1,0:T(8,128)(2,1)} %y_ref.1, f32[1,2048]{1,0:T(1,128)} %bitcast.3, f32[4]{0:T(128)} %lam_ref.1), custom_call_target="tpu_custom_call" | custom-call | tf_op jit(solution)/shard_map/project_and_sum/pallas_call | solution.py:268
  90.8 14.3 %fit.1 = f32[4,512,1024]{2,1,0:T(8,128)} custom-call(bf16[2,512,1024]{2,1,0:T(8,128)(2,1)} %get-tuple-element.9.c_ref, bf16[8,2,256,512]{3,2,1,0:T(8,128)(2,1)} %bitcast.2, f32[2048,128]{1,0:T(8,128)} %get-tuple-element.11.shr_ref, f32[512,128]{1,0:T(8,128)} %get-tuple-element.12.lev_ref, bf16[512,1024]{1,0:T(8,128)(2,1)} %y_ref.1), custom_call_target="tpu_custom_call" | custom-call | tf_op jit(solution)/shard_map/fit/pallas_call | solution.py:303

commit v4 on v3

--- a/solution.py
+++ b/solution.py
@@ -14,7 +14,7 @@
 ROWS = 16
 
 
-WAVE = 6
+WAVE = 4
 
 
 def bit_orders(bits):
@@ -28,9 +28,9 @@
 def exchange_kernel(
     n, nt, nl, halves,
     s_hbm, w_hbm, y_hbm, sing_ref, lam_ref,
-    c_ref, pj_ref, lev_ref, shr_ref,
-    s_ref, w_ref, y_ref, acc, pb, rb,
-    s_sem, w_sem, y_sem, rs_send, rs_recv, ag_send, ag_recv, c_send, c_recv,
+    part_hbm, c_late, p_late, shr_late, lev_ref,
+    s_ref, w_ref, y_ref, acc, pb, rb, c_ref, pj_ref, shr_ref, part, c_wave, scaled,
+    part_sem, s_sem, w_sem, y_sem, rs_send, rs_recv, ag_send, ag_recv, c_send, c_recv,
 ):
     bits = n.bit_length() - 1
     units, unit, cols_of_unit = acc.shape
@@ -215,20 +215,78 @@
                 result = jnp.where(lane == l, sums[l], result)
             lev_ref[here, :] = result
 
-    waves = [range(s, min(s + WAVE, units)) for s in range(0, units, WAVE)]
+    waves = [range(u, min(u + WAVE, units)) for u in range(0, units, WAVE)]
+    last = len(waves) - 1
+
+    def blocks_of(wave):
+        return range(wave[0] // halves, (wave[-1] + 1) // halves)
+
+    def part_copy(l):
+        return pltpu.make_async_copy(part.at[l], part_hbm.at[l], part_sem.at[l])
+
+    def gather_columns(wave, target):
+        for i, s in enumerate(blocks_of(wave)):
+            if own:
+                t = lax.rem(mt + s // own, nt)
+                target[:, i * unit:(i + 1) * unit] = (
+                    c_ref[t, :, (s % own) * unit:(s % own + 1) * unit]
+                )
+            else:
+                pieces = unit // own_k
+                for p in range(pieces):
+                    at = i * unit + p * own_k
+                    target[:, at:at + own_k] = c_ref[s * pieces + p]
+
+    def shrink_rows(s):
+        return pl.ds(pl.multiple_of(lax.div(place(s * halves), halves) * unit, ROWS), unit)
+
+    def fit(w):
+        wave = waves[w]
+        gather_columns(wave, c_wave)
+        for l in range(nl):
+            for h in range(halves):
+                for i, s in enumerate(blocks_of(wave)):
+                    wide = pj_ref[place(s * halves + h)].astype(F32)
+                    scaled[i * unit:(i + 1) * unit, :] = (
+                        shr_ref[shrink_rows(s), l:l + 1] * wide
+                    ).astype(BF16)
+                cols = slice(h * cols_of_unit, (h + 1) * cols_of_unit)
+                term = jnp.dot(c_wave[...], scaled[...], preferred_element_type=F32)
+                if w == 0:
+                    part[l, :, cols] = term
+                else:
+                    part[l, :, cols] = part[l, :, cols] + term
+            if w == last - 1:
+                part_copy(l).start()
+
     for k in range(2 * bits + len(waves)):
         for w, wave in reversed(list(enumerate(waves))):
-            for s in wave:
-                stage = k - w
+            stage = k - w
+            if stage == 2 * bits and w > 0:
+                fit(w - 1)
+            for u in wave:
                 if stage == 0:
-                    begin(s)
+                    begin(u)
                 elif 0 < stage <= bits:
-                    halve(s, stage - 1)
+                    halve(u, stage - 1)
                 elif bits < stage <= 2 * bits:
-                    double(s, 2 * bits - stage)
-        if k == 2 * bits - 1:
+                    double(u, 2 * bits - stage)
+        if k == 2 * bits - 2:
             leverage()
-
+            gather_columns(waves[last], c_late)
+            for i, s in enumerate(blocks_of(waves[last])):
+                shr_late[i * unit:(i + 1) * unit, :] = shr_ref[shrink_rows(s), :]
+            if last == 0:
+                part[...] = jnp.zeros_like(part)
+                for l in range(nl):
+                    part_copy(l).start()
+
+    for i, s in enumerate(blocks_of(waves[last])):
+        for h in range(halves):
+            cols = slice(h * cols_of_unit, (h + 1) * cols_of_unit)
+            p_late[i * unit:(i + 1) * unit, cols] = pj_ref[place(s * halves + h)]
+    for l in range(nl):
+        part_copy(l).wait()
     for d in range(nt - 1):
         c_copy(d).wait_send()
     for s in range(units):
@@ -237,17 +295,12 @@
             ag_copy(s, j).wait_send()
 
 
-def fit_kernel(nl, nt, c_ref, pj_ref, shr_ref, lev_ref, y_ref, out_ref):
-    own_k = c_ref.shape[2]
-    pj = pj_ref[...].reshape(nt * own_k, pj_ref.shape[2])
+def finish_kernel(nl, part_ref, c_ref, p_ref, shr_ref, lev_ref, y_ref, out_ref):
     target = y_ref[...].astype(F32)
+    wide = p_ref[...].astype(F32)
     for l in range(nl):
-        fitted = jnp.zeros(target.shape, F32)
-        for t in range(nt):
-            here = slice(t * own_k, (t + 1) * own_k)
-            wide = pj[here, :].astype(F32)
-            scaled = (shr_ref[here, l:l + 1] * wide).astype(BF16)
-            fitted = fitted + jnp.dot(c_ref[t], scaled, preferred_element_type=F32)
+        scaled = (shr_ref[:, l:l + 1] * wide).astype(BF16)
+        fitted = part_ref[l] + jnp.dot(c_ref[...], scaled, preferred_element_type=F32)
         divisor = jnp.maximum(1.0 - lev_ref[:, l:l + 1], 0.25)
         out_ref[l] = (target - fitted) * (1.0 / divisor)
 
@@ -264,17 +317,20 @@
     blocks = max(own_k // unit, 1)
     rows = k // unit
     units = rows * halves
+    late = ((units - 1) % WAVE + 1) // halves * unit
+    wave_k = WAVE // halves * unit
     vmem = pl.BlockSpec(memory_space=pltpu.VMEM)
-    components, projected, leverage, shrink = pl.pallas_call(
+    partial, components, projected, shrink, leverage = pl.pallas_call(
         functools.partial(exchange_kernel, n, nt, nl, halves),
         out_shape=[
-            jax.ShapeDtypeStruct((nt, tall, own_k), BF16),
-            jax.ShapeDtypeStruct((units, unit, cols), BF16),
+            jax.ShapeDtypeStruct((nl, tall, wide), F32),
+            jax.ShapeDtypeStruct((tall, late), BF16),
+            jax.ShapeDtypeStruct((late, wide), BF16),
+            jax.ShapeDtypeStruct((late, LANES), F32),
             jax.ShapeDtypeStruct((tall, LANES), F32),
-            jax.ShapeDtypeStruct((k, LANES), F32),
         ],
         in_specs=[pl.BlockSpec(memory_space=pl.ANY)] * 3 + [vmem, pl.BlockSpec(memory_space=pltpu.SMEM)],
-        out_specs=[vmem] * 4,
+        out_specs=[pl.BlockSpec(memory_space=pl.ANY)] + [vmem] * 4,
         scratch_shapes=[
             pltpu.VMEM(samples.shape, BF16),
             pltpu.VMEM(whitening.shape, BF16),
@@ -282,6 +338,13 @@
             pltpu.VMEM((units, unit, cols), F32),
             pltpu.VMEM((units, unit, cols), BF16),
             pltpu.VMEM((units, unit, cols), BF16),
+            pltpu.VMEM((nt, tall, own_k), BF16),
+            pltpu.VMEM((units, unit, cols), BF16),
+            pltpu.VMEM((k, LANES), F32),
+            pltpu.VMEM((nl, tall, wide), F32),
+            pltpu.VMEM((tall, wave_k), BF16),
+            pltpu.VMEM((wave_k, cols), BF16),
+            pltpu.SemaphoreType.DMA((nl,)),
             pltpu.SemaphoreType.DMA,
             pltpu.SemaphoreType.DMA((blocks,)),
             pltpu.SemaphoreType.DMA,
@@ -297,24 +360,23 @@
         ),
         name="project_and_sum",
     )(samples, whitening, traits, singular.reshape(1, k), lambdas)
-    projected = projected.reshape(rows, halves, unit, cols)
-    tile = min(256, cols)
-    per = cols // tile
+    tile = min(2 * LANES, wide)
     return pl.pallas_call(
-        functools.partial(fit_kernel, nl, nt),
+        functools.partial(finish_kernel, nl),
         grid=(wide // tile,),
         out_shape=jax.ShapeDtypeStruct((nl, tall, wide), F32),
         in_specs=[
-            pl.BlockSpec((nt, tall, own_k), lambda i: (0, 0, 0)),
-            pl.BlockSpec((rows, None, unit, tile), lambda i: (0, i // per, 0, i % per)),
-            pl.BlockSpec((k, LANES), lambda i: (0, 0)),
+            pl.BlockSpec((nl, tall, tile), lambda i: (0, 0, i)),
+            pl.BlockSpec((tall, late), lambda i: (0, 0)),
+            pl.BlockSpec((late, tile), lambda i: (0, i)),
+            pl.BlockSpec((late, LANES), lambda i: (0, 0)),
             pl.BlockSpec((tall, LANES), lambda i: (0, 0)),
             pl.BlockSpec((tall, tile), lambda i: (0, i)),
         ],
         out_specs=pl.BlockSpec((nl, tall, tile), lambda i: (0, 0, i)),
         compiler_params=pltpu.CompilerParams(vmem_limit_bytes=60 * 2**20),
-        name="fit",
-    )(components, projected, shrink, leverage, traits)
+        name="finish",
+    )(partial, components, projected, shrink, leverage, traits)
 
 
 def solution(mesh):

time: 105 us -> 95.2 us (0.907)
  Pallas kernels: 105 us -> 95 us
    pallas_call x1, Pallas kernels: 90.8 us -> 85.5 us  [local(): pl.pallas_call(functools.partial(exchange_kernel, n, nt, nl, halves), out...]
    pallas_call x1, Pallas kernels: 14.3 us -> 9.43 us  [local(): pl.pallas_call(functools.partial(finish_kernel, nl), grid=(wide // tile,)...]
where the time goes in v4:
time: 95.2 us; the launch traced here: 95 us
  Pallas kernels  95 us (100%)
    pallas_call x1, Pallas kernels, local(): pl.pallas_call(functools.partial(exchange_kernel, n, nt, nl, halves), out...  85.5 us
    pallas_call x1, Pallas kernels, local(): pl.pallas_call(functools.partial(finish_kernel, nl), grid=(wide // tile,)...  9.43 us

profile of v4, /device:TPU:0, one launch (start us, length us, event | category | flops | bytes accessed | tf_op | source)
XLA Modules:
  0.0 95.0 jit_solution(2451590920785305514)
XLA Ops:
  0.0 85.5 %project_and_sum.1 = (f32[4,512,1024]{2,1,0:T(8,128)}, bf16[512,512]{1,0:T(8,128)(2,1)}, bf16[512,1024]{1,0:T(8,128)(2,1)}, f32[512,128]{1,0:T(8,128)}, f32[512,128]{1,0:T(8,128)}) custom-call(bf16[512,2048]{1,0:T(8,128)(2,1)} %s_hbm.1, bf16[2048,1024]{1,0:T(8,128)(2,1)} %w_hbm.1, bf16[512,1024]{1,0:T(8,128)(2,1)} %y_ref.1, f32[1,2048]{1,0:T(1,128)} %bitcast.1, ...), custom_call_target="tpu_custom_call" | custom-call | tf_op jit(solution)/shard_map/project_and_sum/pallas_call | solution.py:323
  85.5 9.4 %finish.1 = f32[4,512,1024]{2,1,0:T(8,128)} custom-call(f32[4,512,1024]{2,1,0:T(8,128)} %get-tuple-element.10.part_ref, bf16[512,512]{1,0:T(8,128)(2,1)} %get-tuple-element.11.c_ref, bf16[512,1024]{1,0:T(8,128)(2,1)} %get-tuple-element.12.p_ref, f32[512,128]{1,0:T(8,128)} %get-tuple-element.13.shr_ref, f32[512,128]{1,0:T(8,128)} %get-tuple-element.14.lev_ref, ...), custom_call_target="tpu_custom_call" | custom-call | tf_op jit(solution)/shard_map/finish/pallas_call | solution.py:364

commit v5 on v4

--- a/solution.py
+++ b/solution.py
@@ -17,12 +17,47 @@
 WAVE = 4
 
 
-def bit_orders(bits):
+EARLY = -99
+
+
+def wave_plan(bits, units):
     rest = list(range(bits))
     if bits < 3:
-        return [rest, rest[::-1]]
-    a, b, c = [0, 1, 2] + rest[3:], [1, 2, 0] + rest[3:], [2, 0, 1] + rest[3:]
-    return [a, b, c] * 5 + [[1, 0, 2] + rest[3:]]
+        orders = [rest, rest[::-1]]
+    else:
+        a, b, c = [0, 1, 2] + rest[3:], [1, 2, 0] + rest[3:], [2, 0, 1] + rest[3:]
+        orders = [a, b, c] * 5 + [[1, 0, 2] + rest[3:]]
+    waves = [list(range(u, min(u + WAVE, units))) for u in range(0, units, WAVE)]
+    plan = []
+    for k in range(2 * bits + len(waves)):
+        for w in reversed(range(len(waves))):
+            if k - w == 2 * bits and w > 0:
+                plan.append(-w)
+            if 0 <= k - w <= 2 * bits:
+                plan += waves[w]
+        if k == 2 * bits - 2:
+            plan.append(EARLY)
+    return [orders[u % len(orders)] for u in range(units)], plan
+
+
+PLANS = {
+    (4, 16): ([
+        [0, 1, 2, 3], [1, 0, 2, 3], [0, 1, 2, 3], [2, 1, 0, 3],
+        [1, 2, 0, 3], [0, 1, 2, 3], [2, 1, 0, 3], [0, 1, 2, 3],
+        [0, 1, 2, 3], [2, 1, 0, 3], [1, 2, 0, 3], [2, 1, 0, 3],
+        [0, 1, 2, 3], [1, 0, 2, 3], [0, 1, 2, 3], [0, 1, 2, 3],
+    ], [
+        0, 1, 2, 3, 4, 5, 6, 0, 1, 7, 8, 9, 2, 10, 4, 5, 11, 12, 7, 3, 2, 0, 13, 4, 1, 10, 14, 5, 2, 7, 0, 8,
+        1, 3, 4, 6, 15, 5, 9, 2, 7, 10, 0, 14, 3, 1, 11, 8, 6, 5, 2, 4, 9, 7, 0, 12, 15, 3, 14, 6, 5, 10, 11,
+        4, 9, 13, 1, 8, 7, 2, 3, 14, 0, 12, 6, 15, 11, 1, 9, 5, 8, 13, 2, 14, 3, 10, 6, 15, 4, 12, 0, 7, 8,
+        1, 11, 14, 13, 9, 15, 6, 10, 3, 8, 11, 5, 14, 7, 13, 9, 4, 15, 1, 12, 10, 6, EARLY, 14, 13, 11, 0,
+        15, 2, 3, 12, 5, 8, 9, 10, -1, 13, 6, 12, 7, 4, 11, 15, -2, 13, 12, 8, 9, 10, 14, 11, -3, 15, 13, 12,
+    ]),
+}
+
+
+def make_plan(bits, units):
+    return PLANS.get((bits, units)) or wave_plan(bits, units)
 
 
 def exchange_kernel(
@@ -38,7 +73,7 @@
     own = own_k // unit
     block = min(unit, own_k)
     blocks = own_k // block
-    orders = bit_orders(bits)
+    orders, plan = make_plan(bits, units)
     me, mt = lax.axis_index("samp"), lax.axis_index("trait")
     value = [lax.rem(lax.div(me, 1 << b), 2) for b in range(bits)]
     peer = [me + (1 - 2 * value[b]) * (1 << b) for b in range(bits)]
@@ -66,7 +101,7 @@
         return pl.ds(pl.multiple_of(start, ROWS), size)
 
     def order(s):
-        return orders[s % len(orders)]
+        return orders[s]
 
     keep, give = [], []
     for s in range(units):
@@ -240,7 +275,7 @@
     def shrink_rows(s):
         return pl.ds(pl.multiple_of(lax.div(place(s * halves), halves) * unit, ROWS), unit)
 
-    def fit(w):
+    def fit(w, first, final):
         wave = waves[w]
         gather_columns(wave, c_wave)
         for l in range(nl):
@@ -252,34 +287,39 @@
                     ).astype(BF16)
                 cols = slice(h * cols_of_unit, (h + 1) * cols_of_unit)
                 term = jnp.dot(c_wave[...], scaled[...], preferred_element_type=F32)
-                if w == 0:
+                if first:
                     part[l, :, cols] = term
                 else:
                     part[l, :, cols] = part[l, :, cols] + term
-            if w == last - 1:
+            if final:
                 part_copy(l).start()
 
-    for k in range(2 * bits + len(waves)):
-        for w, wave in reversed(list(enumerate(waves))):
-            stage = k - w
-            if stage == 2 * bits and w > 0:
-                fit(w - 1)
-            for u in wave:
-                if stage == 0:
-                    begin(u)
-                elif 0 < stage <= bits:
-                    halve(u, stage - 1)
-                elif bits < stage <= 2 * bits:
-                    double(u, 2 * bits - stage)
-        if k == 2 * bits - 2:
-            leverage()
-            gather_columns(waves[last], c_late)
-            for i, s in enumerate(blocks_of(waves[last])):
-                shr_late[i * unit:(i + 1) * unit, :] = shr_ref[shrink_rows(s), :]
-            if last == 0:
-                part[...] = jnp.zeros_like(part)
-                for l in range(nl):
-                    part_copy(l).start()
+    def early():
+        leverage()
+        gather_columns(waves[last], c_late)
+        for i, s in enumerate(blocks_of(waves[last])):
+            shr_late[i * unit:(i + 1) * unit, :] = shr_ref[shrink_rows(s), :]
+        if last == 0:
+            part[...] = jnp.zeros_like(part)
+            for l in range(nl):
+                part_copy(l).start()
+
+    stage = [0] * units
+    fits = 0
+    for u in plan:
+        if u == EARLY:
+            early()
+        elif u < 0:
+            fits += 1
+            fit(-1 - u, fits == 1, fits == last)
+        else:
+            if stage[u] == 0:
+                begin(u)
+            elif stage[u] <= bits:
+                halve(u, stage[u] - 1)
+            else:
+                double(u, 2 * bits - stage[u])
+            stage[u] += 1
 
     for i, s in enumerate(blocks_of(waves[last])):
         for h in range(halves):

time: 95.2 us -> 89.1 us (0.936)
  Pallas kernels: 95 us -> 88.8 us
    pallas_call x1, Pallas kernels: 85.5 us -> 79.4 us  [local(): pl.pallas_call(functools.partial(exchange_kernel, n, nt, nl, halves), out...]
where the time goes in v5:
time: 89.1 us; the launch traced here: 88.8 us
  Pallas kernels  88.8 us (100%)
    pallas_call x1, Pallas kernels, local(): pl.pallas_call(functools.partial(exchange_kernel, n, nt, nl, halves), out...  79.4 us
    pallas_call x1, Pallas kernels, local(): pl.pallas_call(functools.partial(finish_kernel, nl), grid=(wide // tile,)...  9.43 us

profile of v5, /device:TPU:0, one launch (start us, length us, event | category | flops | bytes accessed | tf_op | source)
XLA Modules:
  0.0 88.8 jit_solution(2545170697902056019)
XLA Ops:
  0.0 79.4 %project_and_sum.1 = (f32[4,512,1024]{2,1,0:T(8,128)}, bf16[512,512]{1,0:T(8,128)(2,1)}, bf16[512,1024]{1,0:T(8,128)(2,1)}, f32[512,128]{1,0:T(8,128)}, f32[512,128]{1,0:T(8,128)}) custom-call(bf16[512,2048]{1,0:T(8,128)(2,1)} %s_hbm.1, bf16[2048,1024]{1,0:T(8,128)(2,1)} %w_hbm.1, bf16[512,1024]{1,0:T(8,128)(2,1)} %y_ref.1, f32[1,2048]{1,0:T(1,128)} %bitcast.1, ...), custom_call_target="tpu_custom_call" | custom-call | tf_op jit(solution)/shard_map/project_and_sum/pallas_call | solution.py:363
  79.4 9.4 %finish.1 = f32[4,512,1024]{2,1,0:T(8,128)} custom-call(f32[4,512,1024]{2,1,0:T(8,128)} %get-tuple-element.10.part_ref, bf16[512,512]{1,0:T(8,128)(2,1)} %get-tuple-element.11.c_ref, bf16[512,1024]{1,0:T(8,128)(2,1)} %get-tuple-element.12.p_ref, f32[512,128]{1,0:T(8,128)} %get-tuple-element.13.shr_ref, f32[512,128]{1,0:T(8,128)} %get-tuple-element.14.lev_ref, ...), custom_call_target="tpu_custom_call" | custom-call | tf_op jit(solution)/shard_map/finish/pallas_call | solution.py:404

commit v6 on v5

--- a/solution.py
+++ b/solution.py
@@ -63,7 +63,7 @@
 def exchange_kernel(
     n, nt, nl, halves,
     s_hbm, w_hbm, y_hbm, sing_ref, lam_ref,
-    part_hbm, c_late, p_late, shr_late, lev_ref,
+    part_hbm, c_late, p_late, shr_late, inv_ref,
     s_ref, w_ref, y_ref, acc, pb, rb, c_ref, pj_ref, shr_ref, part, c_wave, scaled,
     part_sem, s_sem, w_sem, y_sem, rs_send, rs_recv, ag_send, ag_recv, c_send, c_recv,
 ):
@@ -248,7 +248,7 @@
             result = jnp.zeros((step, LANES), F32)
             for l in range(nl):
                 result = jnp.where(lane == l, sums[l], result)
-            lev_ref[here, :] = result
+            inv_ref[here, :] = 1.0 / jnp.maximum(1.0 - result, 0.25)
 
     waves = [range(u, min(u + WAVE, units)) for u in range(0, units, WAVE)]
     last = len(waves) - 1
@@ -287,10 +287,9 @@
                     ).astype(BF16)
                 cols = slice(h * cols_of_unit, (h + 1) * cols_of_unit)
                 term = jnp.dot(c_wave[...], scaled[...], preferred_element_type=F32)
-                if first:
-                    part[l, :, cols] = term
-                else:
-                    part[l, :, cols] = part[l, :, cols] + term
+                base = y_ref[:, cols].astype(F32) if first else part[l, :, cols]
+                rest = base - term
+                part[l, :, cols] = rest * inv_ref[:, l:l + 1] if final else rest
             if final:
                 part_copy(l).start()
 
@@ -300,8 +299,8 @@
         for i, s in enumerate(blocks_of(waves[last])):
             shr_late[i * unit:(i + 1) * unit, :] = shr_ref[shrink_rows(s), :]
         if last == 0:
-            part[...] = jnp.zeros_like(part)
             for l in range(nl):
+                part[l] = y_ref[...].astype(F32) * inv_ref[:, l:l + 1]
                 part_copy(l).start()
 
     stage = [0] * units
@@ -335,14 +334,12 @@
             ag_copy(s, j).wait_send()
 
 
-def finish_kernel(nl, part_ref, c_ref, p_ref, shr_ref, lev_ref, y_ref, out_ref):
-    target = y_ref[...].astype(F32)
+def finish_kernel(nl, part_ref, c_ref, p_ref, shr_ref, inv_ref, out_ref):
     wide = p_ref[...].astype(F32)
     for l in range(nl):
         scaled = (shr_ref[:, l:l + 1] * wide).astype(BF16)
-        fitted = part_ref[l] + jnp.dot(c_ref[...], scaled, preferred_element_type=F32)
-        divisor = jnp.maximum(1.0 - lev_ref[:, l:l + 1], 0.25)
-        out_ref[l] = (target - fitted) * (1.0 / divisor)
+        fitted = jnp.dot(c_ref[...], scaled, preferred_element_type=F32)
+        out_ref[l] = part_ref[l] - fitted * inv_ref[:, l:l + 1]
 
 
 def local(n, nt, samples, traits, whitening, singular, lambdas):
@@ -360,7 +357,7 @@
     late = ((units - 1) % WAVE + 1) // halves * unit
     wave_k = WAVE // halves * unit
     vmem = pl.BlockSpec(memory_space=pltpu.VMEM)
-    partial, components, projected, shrink, leverage = pl.pallas_call(
+    partial, components, projected, shrink, inverse = pl.pallas_call(
         functools.partial(exchange_kernel, n, nt, nl, halves),
         out_shape=[
             jax.ShapeDtypeStruct((nl, tall, wide), F32),
@@ -411,12 +408,11 @@
             pl.BlockSpec((late, tile), lambda i: (0, i)),
             pl.BlockSpec((late, LANES), lambda i: (0, 0)),
             pl.BlockSpec((tall, LANES), lambda i: (0, 0)),
-            pl.BlockSpec((tall, tile), lambda i: (0, i)),
         ],
         out_specs=pl.BlockSpec((nl, tall, tile), lambda i: (0, 0, i)),
         compiler_params=pltpu.CompilerParams(vmem_limit_bytes=60 * 2**20),
         name="finish",
-    )(partial, components, projected, shrink, leverage, traits)
+    )(partial, components, projected, shrink, inverse)
 
 
 def solution(mesh):

time: 89.1 us -> 88.8 us (level)
  no operation moved by 1% of the time
where the time goes in v6:
time: 88.8 us; the launch traced here: 88.6 us
  Pallas kernels  88.6 us (100%)
    pallas_call x1, Pallas kernels, local(): pl.pallas_call(functools.partial(exchange_kernel, n, nt, nl, halves), out...  79.4 us
    pallas_call x1, Pallas kernels, local(): pl.pallas_call(functools.partial(finish_kernel, nl), grid=(wide // tile,)...  9.17 us

profile of v6, /device:TPU:0, one launch (start us, length us, event | category | flops | bytes accessed | tf_op | source)
XLA Modules:
  0.0 88.6 jit_solution(8100271709787719303)
XLA Ops:
  0.0 79.4 %project_and_sum.1 = (f32[4,512,1024]{2,1,0:T(8,128)}, bf16[512,512]{1,0:T(8,128)(2,1)}, bf16[512,1024]{1,0:T(8,128)(2,1)}, f32[512,128]{1,0:T(8,128)}, f32[512,128]{1,0:T(8,128)}) custom-call(bf16[512,2048]{1,0:T(8,128)(2,1)} %s_hbm.1, bf16[2048,1024]{1,0:T(8,128)(2,1)} %w_hbm.1, bf16[512,1024]{1,0:T(8,128)(2,1)} %y_hbm.1, f32[1,2048]{1,0:T(1,128)} %bitcast.1, ...), custom_call_target="tpu_custom_call" | custom-call | tf_op jit(solution)/shard_map/project_and_sum/pallas_call | solution.py:360
  79.4 9.2 %finish.1 = f32[4,512,1024]{2,1,0:T(8,128)} custom-call(f32[4,512,1024]{2,1,0:T(8,128)} %get-tuple-element.10.part_ref, bf16[512,512]{1,0:T(8,128)(2,1)} %get-tuple-element.11.c_ref, bf16[512,1024]{1,0:T(8,128)(2,1)} %get-tuple-element.12.p_ref, f32[512,128]{1,0:T(8,128)} %get-tuple-element.13.shr_ref, f32[512,128]{1,0:T(8,128)} %get-tuple-element.14.inv_ref), custom_call_target="tpu_custom_call" | custom-call | tf_op jit(solution)/shard_map/finish/pallas_call | solution.py:401
